TPU v7x, 512 devices: a whole 4x8x8 slice. The times are simulated.
512 devices in a mesh: tm: 16 (over y, core), space: 32 (over x, z).
Axes of the slice: x: 4, y: 8, z: 8, core: 2. Of those that a mesh axis runs over, the one named last changes fastest.
Arguments:
- video: bfloat16 [64, 32, 6, 20, 128], P('tm', 'space')
- conv_weight: bfloat16 [3, 3, 3, 3, 128, 128], replicated, may hold values from -0.109375 to 0.109375
- norm_gain: float32 [2, 128], replicated, may hold values from 0.1 to 1.9
- norm_bias: float32 [2, 128], replicated, may hold values from -3 to 3
Outputs:
- latent: bfloat16 [64, 32, 6, 20, 128], P('tm', 'space')
All inputs are finite; a program needn't handle non-finite values.
Results may differ from a plain program's by a relative error of at most 0.006.
Values may be sent and summed in bfloat16 or wider, within the bound.
A program may use at most 64 MiB of HBM per device.

v0:
```python
import jax
import jax.numpy as jnp
from jax import lax
from jax.sharding import PartitionSpec as P

GROUPS = 32
TILE_COLS = 8
LAYERS = 3


EPS = 1e-05


def shifted(value, axis, steps):
    count = lax.axis_size(axis)
    leading, last = (max(0, -steps), min(count, count - steps))
    return lax.ppermute(value, axis, [(source, source + steps) for source in range(leading, last)])


def taps(block, weight):
    frames = block.shape[0] - 2
    rows = block.shape[1] - 2
    width = block.shape[2] - 2
    chans = block.shape[3]
    kernel = weight.reshape(3, 3, 3 * chans, chans)
    total = jnp.zeros((frames * rows * width, chans), jnp.float32)
    for step_t in range(3):
        for step_r in range(3):
            columns = jnp.concatenate(
                [
                    block[step_t : step_t + frames, step_r : step_r + rows, step_c : step_c + width]
                    for step_c in range(3)
                ],
                axis=-1,
            )
            total = total + jnp.dot(
                columns.reshape(-1, 3 * chans),
                kernel[step_t, step_r],
                preferred_element_type=jnp.float32,
            )
    return total.reshape(frames, rows, width, chans)


def rims(block):
    column = lax.axis_index("space") % TILE_COLS
    upper = shifted(block[:, -1:], "space", TILE_COLS)
    lower = shifted(block[:, :1], "space", -TILE_COLS)
    tall = jnp.concatenate([upper, block, lower], axis=1)
    left_side = shifted(tall[:, :, -1:], "space", 1)
    right_side = shifted(tall[:, :, :1], "space", -1)
    left_side = jnp.where(column == 0, jnp.zeros_like(left_side), left_side)
    right_side = jnp.where(column == TILE_COLS - 1, jnp.zeros_like(right_side), right_side)
    return jnp.concatenate([left_side, tall, right_side], axis=2)


def extend(current):
    cache = shifted(current[-2:], "tm", 1)
    joined = jnp.concatenate([cache, current], axis=0)
    return rims(joined)


def group_sums(values, per):
    frames = values.shape[0]
    return jnp.sum(values, axis=(1, 2)).reshape(frames, GROUPS, per).sum(-1)


def group_norm(result, gain, bias):
    frames, rows, width, chans = result.shape
    per = chans // GROUPS
    count = rows * width * per * lax.axis_size("space")
    mean = lax.psum(group_sums(result, per), "space") / count
    mean_c = jnp.repeat(mean, per, axis=1)[:, None, None, :]
    centered = result - mean_c
    var = lax.psum(group_sums(centered * centered, per), "space") / count
    scale_c = jnp.repeat(lax.rsqrt(var + EPS), per, axis=1)[:, None, None, :]
    return jax.nn.silu((result - mean_c) * scale_c * gain + bias).astype(jnp.bfloat16)


def on_device(video, conv_weight, norm_gain, norm_bias):
    current = video[:, 0]
    for layer in range(LAYERS):
        result = taps(extend(current), conv_weight[layer])
        if layer == LAYERS - 1:
            current = result.astype(jnp.bfloat16)
        else:
            current = group_norm(result, norm_gain[layer], norm_bias[layer])
    return current[:, None]


def solution(mesh):
    placed = (P("tm", "space", None, None, None), P(), P(), P())
    return jax.shard_map(
        on_device,
        mesh=mesh,
        in_specs=placed,
        out_specs=P("tm", "space", None, None, None),
        check_vma=False,
    )
```

profile of v0, /device:TPU:1, one launch (start us, length us, event | category | flops | bytes accessed | tf_op | source)
XLA Modules:
  0.0 418.8 jit_solution(7379829779001315549)
XLA Ops:
  1.0 4.6 %collective-permute-start = (bf16[2,6,20,128]{3,2,1,0:T(8,128)(2,1)S(1)}, bf16[2,6,20,128]{3,2,1,0:T(8,128)(2,1)S(1)}, u32[]{:S(2)}, u32[]{:S(2)}) collective-permute-start(bf16[2,6,20,128]{3,2,1,0:T(8,128)(2,1)S(1)} %slice_bitcast_fusion.54), channel_id=1, source_target_pairs={{0,32},{32,64},{64,96},{96,128},{128,160},{160,192},{192,224},{224... | collective-permute-start | bytes 184328 | tf_op jit(solution)/shard_map/ppermute | solution.py:17
  5.6 2.0 fusion.19
  8.3 1.5 collective-permute-done
  9.9 1.6 collective-permute-start.1
  11.5 1.3 collective-permute-start.2
  13.5 2.7 collective-permute-done.2
  16.2 4.0 collective-permute-start.3
  20.3 1.3 collective-permute-start.4
  22.6 2.9 collective-permute-done.4
  25.7 1.5 fusion.24
  28.2 1.6 concatenate.218
  29.7 1.6 concatenate.220
  44.4 1.4 convolution_add_fusion.23
  49.0 62.3 %psum.28 = f32[4,32]{1,0:T(4,128)S(1)} all-reduce(f32[4,32]{1,0:T(4,128)S(1)} %reduce_sum.73), channel_id=1, replica_groups=mesh['tm'=16,'space'=32] {'space'}, use_global_device_ids=true, to_apply=%region_2.3 | all-reduce | flops 128 | bytes 1024 | tf_op jit(solution)/shard_map/psum | solution.py:71
  111.8 56.2 %psum.29 = f32[4,32]{1,0:T(4,128)S(1)} all-reduce(f32[4,32]{1,0:T(4,128)S(1)} %reduce_sum.75), channel_id=1, replica_groups=mesh['tm'=16,'space'=32] {'space'}, use_global_device_ids=true, to_apply=%region_5.6 | all-reduce | flops 128 | bytes 1024 | tf_op jit(solution)/shard_map/psum | solution.py:74
  168.4 32.6 %collective-permute-start.5 = (bf16[2,6,20,128]{3,2,1,0:T(8,128)(2,1)S(1)}, bf16[2,6,20,128]{3,2,1,0:T(8,128)(2,1)S(1)}, u32[]{:S(2)}, u32[]{:S(2)}) collective-permute-start(bf16[2,6,20,128]{3,2,1,0:T(8,128)(2,1)S(1)} %slice.620), channel_id=1, source_target_pairs={{0,32},{32,64},{64,96},{96,128},{128,160},{160,192},{192,224},{224... | collective-permute-start | bytes 184328 | tf_op jit(solution)/shard_map/ppermute | solution.py:17
  201.0 1.4 collective-permute-done.5
  202.4 1.3 collective-permute-start.6
  203.7 1.3 collective-permute-start.7
  205.0 3.4 collective-permute-done.7
  208.5 3.6 collective-permute-start.8
  213.7 3.0 collective-permute-done.9
  237.4 55.8 %psum.30 = f32[4,32]{1,0:T(4,128)S(1)} all-reduce(f32[4,32]{1,0:T(4,128)S(1)} %reduce_sum.77), channel_id=1, replica_groups=mesh['tm'=16,'space'=32] {'space'}, use_global_device_ids=true, to_apply=%region_8.9 | all-reduce | flops 128 | bytes 1024 | tf_op jit(solution)/shard_map/psum | solution.py:71
  293.7 58.0 %psum.31 = f32[4,32]{1,0:T(4,128)S(1)} all-reduce(f32[4,32]{1,0:T(4,128)S(1)} %reduce_sum.79), channel_id=1, replica_groups=mesh['tm'=16,'space'=32] {'space'}, use_global_device_ids=true, to_apply=%region_11.12 | all-reduce | flops 128 | bytes 1024 | tf_op jit(solution)/shard_map/psum | solution.py:74
  352.0 34.4 %collective-permute-start.10 = (bf16[2,6,20,128]{3,2,1,0:T(8,128)(2,1)S(1)}, bf16[2,6,20,128]{3,2,1,0:T(8,128)(2,1)S(1)}, u32[]{:S(2)}, u32[]{:S(2)}) collective-permute-start(bf16[2,6,20,128]{3,2,1,0:T(8,128)(2,1)S(1)} %slice.656), channel_id=1, source_target_pairs={{0,32},{32,64},{64,96},{96,128},{128,160},{160,192},{192,224},{224... | collective-permute-start | bytes 184328 | tf_op jit(solution)/shard_map/ppermute | solution.py:17
  386.4 1.4 collective-permute-done.10
  387.8 1.3 collective-permute-start.11
  389.1 1.3 collective-permute-start.12
  390.4 3.4 collective-permute-done.12
  393.8 1.7 collective-permute-start.13
  395.5 1.5 collective-permute-start.14
  397.2 2.8 collective-permute-done.14
  (197 shorter events, 63.2 us)
Async XLA Ops:
  0.9 6.7 %copy-start.22 = (f32[2,128]{1,0:T(2,128)S(1)}, f32[2,128]{1,0:T(2,128)}, u32[]{:S(2)}) copy-start(f32[2,128]{1,0:T(2,128)} %param.7) | copy-start | bytes 3076
  1.0 6.7 %copy-start.23 = (f32[2,128]{1,0:T(2,128)S(1)}, f32[2,128]{1,0:T(2,128)}, u32[]{:S(2)}) copy-start(f32[2,128]{1,0:T(2,128)} %param.6) | copy-start | bytes 3076
  1.0 8.9 %collective-permute-start = (bf16[2,6,20,128]{3,2,1,0:T(8,128)(2,1)S(1)}, bf16[2,6,20,128]{3,2,1,0:T(8,128)(2,1)S(1)}, u32[]{:S(2)}, u32[]{:S(2)}) collective-permute-start(bf16[2,6,20,128]{3,2,1,0:T(8,128)(2,1)S(1)} %slice_bitcast_fusion.54), channel_id=1, source_target_pairs={{0,32},{32,64},{64,96},{96,128},{128,160},{160,192},{192,224},{224... | collective-permute-start | bytes 184328 | tf_op jit(solution)/shard_map/ppermute | solution.py:17
  9.9 3.6 collective-permute-start.1
  11.5 4.7 %collective-permute-start.2 = (bf16[6,1,20,128]{3,2,1,0:T(8,128)(2,1)S(1)}, bf16[6,1,20,128]{3,2,1,0:T(8,128)(2,1)S(1)}, u32[]{:S(2)}, u32[]{:S(2)}) collective-permute-start(bf16[6,1,20,128]{3,2,1,0:T(8,128)(2,1)S(1)} %get-tuple-element.103), channel_id=1, source_target_pairs={{8,0},{9,1},{10,2},{11,3},{12,4},{13,5},{14,6},{15,7},{16,8},{17,9... | collective-permute-start | bytes 92168 | tf_op jit(solution)/shard_map/ppermute | solution.py:17
  16.2 6.3 %collective-permute-start.3 = (bf16[6,8,1,128]{3,2,1,0:T(2,128)(2,1)S(1)}, bf16[6,8,1,128]{3,2,1,0:T(2,128)(2,1)S(1)}, u32[]{:S(2)}, u32[]{:S(2)}) collective-permute-start(bf16[6,8,1,128]{3,2,1,0:T(2,128)(2,1)S(1)} %get-tuple-element.72), channel_id=1, source_target_pairs={{0,1},{1,2},{2,3},{3,4},{4,5},{5,6},{6,7},{7,8},{8,9},{9,10},{10,1... | collective-permute-start | bytes 36872 | tf_op jit(solution)/shard_map/ppermute | solution.py:17
  20.3 5.2 %collective-permute-start.4 = (bf16[6,8,1,128]{3,2,1,0:T(2,128)(2,1)S(1)}, bf16[6,8,1,128]{3,2,1,0:T(2,128)(2,1)S(1)}, u32[]{:S(2)}, u32[]{:S(2)}) collective-permute-start(bf16[6,8,1,128]{3,2,1,0:T(2,128)(2,1)S(1)} %get-tuple-element.73), channel_id=1, source_target_pairs={{1,0},{2,1},{3,2},{4,3},{5,4},{6,5},{7,6},{8,7},{9,8},{10,9},{11,1... | collective-permute-start | bytes 36872 | tf_op jit(solution)/shard_map/ppermute | solution.py:17
  33.2 6.0 %copy-start.12 = (bf16[4,6,20,128]{3,2,1,0:T(8,128)(2,1)S(1)}, bf16[4,6,20,128]{3,2,1,0:T(8,128)(2,1)}, u32[]{:S(2)}) copy-start(bf16[4,6,20,128]{3,2,1,0:T(8,128)(2,1)} %get-tuple-element.88) | copy-start | bytes 368644
  35.2 5.9 %copy-start.13 = (bf16[4,6,20,128]{3,2,1,0:T(8,128)(2,1)S(1)}, bf16[4,6,20,128]{3,2,1,0:T(8,128)(2,1)}, u32[]{:S(2)}) copy-start(bf16[4,6,20,128]{3,2,1,0:T(8,128)(2,1)} %fusion.14) | copy-start | bytes 368644
  37.2 5.8 %copy-start.11 = (bf16[4,6,20,128]{3,2,1,0:T(8,128)(2,1)S(1)}, bf16[4,6,20,128]{3,2,1,0:T(8,128)(2,1)}, u32[]{:S(2)}) copy-start(bf16[4,6,20,128]{3,2,1,0:T(8,128)(2,1)} %get-tuple-element.123) | copy-start | bytes 368644
  44.4 3.8 copy-start.19
  44.4 3.8 copy-start.20
  168.4 34.0 %collective-permute-start.5 = (bf16[2,6,20,128]{3,2,1,0:T(8,128)(2,1)S(1)}, bf16[2,6,20,128]{3,2,1,0:T(8,128)(2,1)S(1)}, u32[]{:S(2)}, u32[]{:S(2)}) collective-permute-start(bf16[2,6,20,128]{3,2,1,0:T(8,128)(2,1)S(1)} %slice.620), channel_id=1, source_target_pairs={{0,32},{32,64},{64,96},{96,128},{128,160},{160,192},{192,224},{224... | collective-permute-start | bytes 184328 | tf_op jit(solution)/shard_map/ppermute | solution.py:17
  202.4 2.6 collective-permute-start.6
  203.7 4.7 %collective-permute-start.7 = (bf16[6,1,20,128]{3,2,1,0:T(8,128)(2,1)S(1)}, bf16[6,1,20,128]{3,2,1,0:T(8,128)(2,1)S(1)}, u32[]{:S(2)}, u32[]{:S(2)}) collective-permute-start(bf16[6,1,20,128]{3,2,1,0:T(8,128)(2,1)S(1)} %get-tuple-element.99), channel_id=1, source_target_pairs={{8,0},{9,1},{10,2},{11,3},{12,4},{13,5},{14,6},{15,7},{16,8},{17,9... | collective-permute-start | bytes 92168 | tf_op jit(solution)/shard_map/ppermute | solution.py:17
  208.5 5.2 %collective-permute-start.8 = (bf16[6,8,1,128]{3,2,1,0:T(2,128)(2,1)S(1)}, bf16[6,8,1,128]{3,2,1,0:T(2,128)(2,1)S(1)}, u32[]{:S(2)}, u32[]{:S(2)}) collective-permute-start(bf16[6,8,1,128]{3,2,1,0:T(2,128)(2,1)S(1)} %get-tuple-element.50), channel_id=1, source_target_pairs={{0,1},{1,2},{2,3},{3,4},{4,5},{5,6},{6,7},{7,8},{8,9},{9,10},{10,1... | collective-permute-start | bytes 36872 | tf_op jit(solution)/shard_map/ppermute | solution.py:17
  212.1 4.6 %collective-permute-start.9 = (bf16[6,8,1,128]{3,2,1,0:T(2,128)(2,1)S(1)}, bf16[6,8,1,128]{3,2,1,0:T(2,128)(2,1)S(1)}, u32[]{:S(2)}, u32[]{:S(2)}) collective-permute-start(bf16[6,8,1,128]{3,2,1,0:T(2,128)(2,1)S(1)} %get-tuple-element.51), channel_id=1, source_target_pairs={{1,0},{2,1},{3,2},{4,3},{5,4},{6,5},{7,6},{8,7},{9,8},{10,9},{11,1... | collective-permute-start | bytes 36872 | tf_op jit(solution)/shard_map/ppermute | solution.py:17
  221.8 5.7 %copy-start.15 = (bf16[4,6,20,128]{3,2,1,0:T(8,128)(2,1)S(1)}, bf16[4,6,20,128]{3,2,1,0:T(8,128)(2,1)}, u32[]{:S(2)}) copy-start(bf16[4,6,20,128]{3,2,1,0:T(8,128)(2,1)} %get-tuple-element.37) | copy-start | bytes 368644
  223.7 5.6 %copy-start.17 = (bf16[4,6,20,128]{3,2,1,0:T(8,128)(2,1)S(1)}, bf16[4,6,20,128]{3,2,1,0:T(8,128)(2,1)}, u32[]{:S(2)}) copy-start(bf16[4,6,20,128]{3,2,1,0:T(8,128)(2,1)} %get-tuple-element.47) | copy-start | bytes 368644
  231.6 4.5 %copy-start.4 = (bf16[480,384]{1,0:T(8,128)(2,1)S(1)}, bf16[480,384]{1,0:T(8,128)(2,1)}, u32[]{:S(2)}) copy-start(bf16[480,384]{1,0:T(8,128)(2,1)} %reshape.138) | copy-start | bytes 1105924
  231.6 4.7 %copy-start.2 = (bf16[480,384]{1,0:T(8,128)(2,1)S(1)}, bf16[480,384]{1,0:T(8,128)(2,1)}, u32[]{:S(2)}) copy-start(bf16[480,384]{1,0:T(8,128)(2,1)} %reshape.139) | copy-start | bytes 1105924
  231.9 4.7 %copy-start.10 = (bf16[480,384]{1,0:T(8,128)(2,1)S(1)}, bf16[480,384]{1,0:T(8,128)(2,1)}, u32[]{:S(2)}) copy-start(bf16[480,384]{1,0:T(8,128)(2,1)} %reshape.140) | copy-start | bytes 1105924
  352.0 35.8 %collective-permute-start.10 = (bf16[2,6,20,128]{3,2,1,0:T(8,128)(2,1)S(1)}, bf16[2,6,20,128]{3,2,1,0:T(8,128)(2,1)S(1)}, u32[]{:S(2)}, u32[]{:S(2)}) collective-permute-start(bf16[2,6,20,128]{3,2,1,0:T(8,128)(2,1)S(1)} %slice.656), channel_id=1, source_target_pairs={{0,32},{32,64},{64,96},{96,128},{128,160},{160,192},{192,224},{224... | collective-permute-start | bytes 184328 | tf_op jit(solution)/shard_map/ppermute | solution.py:17
  387.8 2.6 collective-permute-start.11
  389.1 4.7 %collective-permute-start.12 = (bf16[6,1,20,128]{3,2,1,0:T(8,128)(2,1)S(1)}, bf16[6,1,20,128]{3,2,1,0:T(8,128)(2,1)S(1)}, u32[]{:S(2)}, u32[]{:S(2)}) collective-permute-start(bf16[6,1,20,128]{3,2,1,0:T(8,128)(2,1)S(1)} %get-tuple-element.95), channel_id=1, source_target_pairs={{8,0},{9,1},{10,2},{11,3},{12,4},{13,5},{14,6},{15,7},{16,8},{17,9... | collective-permute-start | bytes 92168 | tf_op jit(solution)/shard_map/ppermute | solution.py:17
  393.8 3.4 collective-permute-start.13
  395.5 4.6 %collective-permute-start.14 = (bf16[6,8,1,128]{3,2,1,0:T(2,128)(2,1)S(1)}, bf16[6,8,1,128]{3,2,1,0:T(2,128)(2,1)S(1)}, u32[]{:S(2)}, u32[]{:S(2)}) collective-permute-start(bf16[6,8,1,128]{3,2,1,0:T(2,128)(2,1)S(1)} %get-tuple-element.29), channel_id=1, source_target_pairs={{1,0},{2,1},{3,2},{4,3},{5,4},{6,5},{7,6},{8,7},{9,8},{10,9},{11,1... | collective-permute-start | bytes 36872 | tf_op jit(solution)/shard_map/ppermute | solution.py:17
  402.8 5.7 %copy-start.16 = (bf16[4,6,20,128]{3,2,1,0:T(8,128)(2,1)S(1)}, bf16[4,6,20,128]{3,2,1,0:T(8,128)(2,1)}, u32[]{:S(2)}) copy-start(bf16[4,6,20,128]{3,2,1,0:T(8,128)(2,1)} %get-tuple-element.15) | copy-start | bytes 368644
  404.7 5.6 %copy-start.14 = (bf16[4,6,20,128]{3,2,1,0:T(8,128)(2,1)S(1)}, bf16[4,6,20,128]{3,2,1,0:T(8,128)(2,1)}, u32[]{:S(2)}) copy-start(bf16[4,6,20,128]{3,2,1,0:T(8,128)(2,1)} %get-tuple-element.16) | copy-start | bytes 368644
  404.7 5.6 %copy-start.18 = (bf16[4,6,20,128]{3,2,1,0:T(8,128)(2,1)S(1)}, bf16[4,6,20,128]{3,2,1,0:T(8,128)(2,1)}, u32[]{:S(2)}) copy-start(bf16[4,6,20,128]{3,2,1,0:T(8,128)(2,1)} %get-tuple-element.25) | copy-start | bytes 368644
  412.6 4.4 %copy-start.3 = (bf16[480,384]{1,0:T(8,128)(2,1)S(1)}, bf16[480,384]{1,0:T(8,128)(2,1)}, u32[]{:S(2)}) copy-start(bf16[480,384]{1,0:T(8,128)(2,1)} %reshape.150) | copy-start | bytes 1105924
  412.9 4.6 %copy-start.9 = (bf16[480,384]{1,0:T(8,128)(2,1)S(1)}, bf16[480,384]{1,0:T(8,128)(2,1)}, u32[]{:S(2)}) copy-start(bf16[480,384]{1,0:T(8,128)(2,1)} %reshape.152) | copy-start | bytes 1105924
  (7 other events, 22.5 us)
where the time goes:
time: 426 us; the launch traced here: 419 us
  blocking collectives  232 us (54%)
  starting transfers between devices  93 us (22%)
  local copies, waits for them, and re-layouts  32 us (8%)
  other arithmetic  22.9 us (5%)
  waiting for transfers between devices  22.5 us (5%)
  matrix products  15.2 us (4%)
    psum x2, blocking collectives, group_norm(): mean = lax.psum(group_sums(result, per), 'space') / count  118 us
    psum x2, blocking collectives, group_norm(): var = lax.psum(group_sums(centered * centered, per), 'space') / count  114 us
    ppermute x15, starting transfers between devices, shifted(): lax.ppermute(value, axis, [(source, source + steps) for source in range(l...  93 us
    ppermute x15, waiting for transfers between devices, shifted(): lax.ppermute(value, axis, [(source, source + steps) for source in range(l...  22.5 us
    concatenate x24, other arithmetic, taps(): jnp.concatenate([block[step_t:step_t + frames, step_r:step_r + rows, step...  20.1 us
    reshape x26, local copies, waits for them, and re-layouts, taps(): columns.reshape(-1, 3 * chans)  16.2 us
    dot_general x27, matrix products, taps(): jnp.dot(columns.reshape(-1, 3 * chans), kernel[step_t, step_r], preferred...  15.2 us
  transfers between devices with their start and end apart: 15, of which 9 were waited for; matrix products, arithmetic and copies ran while one was open for 1% of the time, Pallas kernels for 0%

commit v1 on v0

v1 whole, which is shorter than its diff:
```python
import jax
import jax.numpy as jnp
from jax import lax
from jax.experimental import pallas as pl
from jax.experimental.pallas import tpu as pltpu
from jax.sharding import PartitionSpec as P

GROUPS = 32
TILE_COLS = 8
BANDS = 4
LAYERS = 3
EPS = 1e-05
F32 = jnp.float32
BF16 = jnp.bfloat16
MESH = pl.DeviceIdType.MESH

FR = 4
TH = 6
TW = 20
C = 128
CELLS = TH * TW
ROWS = 128
PAD = 8
XROWS = PAD + (TH + 2) * TW + 8
K = 9 * C
COUNT = BANDS * TH * TILE_COLS * TW * (C // GROUPS)


def dot(left, right):
    return jnp.dot(left, right, preferred_element_type=F32)


def pack_sums(total):
    lane = lax.broadcasted_iota(jnp.int32, (1, C), 1) % 4
    pair = total + pltpu.roll(total, 1, 1)
    quad = pair + pltpu.roll(pair, 2, 1)
    first = jnp.zeros((1, C), F32)
    second = jnp.zeros((1, C), F32)
    for f in range(FR):
        moved = quad if f == 3 else pltpu.roll(quad, C - (3 - f), 1)
        first = jnp.where(lane == f, moved[f : f + 1], first)
        second = jnp.where(lane == f, moved[4 + f : 5 + f], second)
    return jnp.concatenate([first, second], axis=0)


def unpack_sums(packed):
    lane = lax.broadcasted_iota(jnp.int32, (8, C), 1) % 4
    row = lax.broadcasted_iota(jnp.int32, (8, C), 0)
    spread = jnp.where(row < 4, packed[0:1], packed[1:2])
    only = jnp.where(lane == row % 4, spread, 0.0)
    lead = jnp.where(row % 4 == 0, only, 0.0)
    for f in range(1, FR):
        lead = jnp.where(row % 4 == f, pltpu.roll(only, C - f, 1), lead)
    pair = lead + pltpu.roll(lead, 1, 1)
    return pair + pltpu.roll(pair, 2, 1)


def moments(packed, gain):
    sums = unpack_sums(packed) * (1.0 / COUNT)
    mean = sums[0:4]
    var = sums[4:8] - mean * mean
    return mean, lax.rsqrt(var + EPS) * gain


def kernel(
    video,
    weights,
    gain_in,
    bias_in,
    out,
    w,
    vid,
    gains,
    biases,
    y,
    acc,
    xc,
    im,
    cols,
    corners,
    rim,
    rim_corner,
    halo,
    halo_rim,
    halo_corner,
    packed,
    slots,
    prev_slots,
    load_sem,
    send_sem,
    recv_sem,
    stat_send,
    stat_recv,
):
    tm = lax.axis_index("tm")
    space = lax.axis_index("space")
    n_tm = lax.axis_size("tm")
    n_space = lax.axis_size("space")
    band = space // TILE_COLS
    column = space % TILE_COLS
    up = lax.rem(band + BANDS - 1, BANDS)
    down = lax.rem(band + 1, BANDS)
    left = lax.rem(column + TILE_COLS - 1, TILE_COLS)
    right = lax.rem(column + 1, TILE_COLS)
    after = lax.rem(tm + 1, n_tm)
    before = lax.rem(tm + n_tm - 1, n_tm)

    loads = [pltpu.make_async_copy(video, vid, load_sem.at[0])]
    for layer in range(LAYERS):
        loads.append(pltpu.make_async_copy(weights.at[layer], w.at[layer], load_sem.at[1 + layer]))
    loads.append(pltpu.make_async_copy(gain_in, gains, load_sem.at[4]))
    loads.append(pltpu.make_async_copy(bias_in, biases, load_sem.at[5]))
    for copy in loads:
        copy.start()

    barrier = pltpu.get_barrier_semaphore()

    def greet(d, carry):
        pl.semaphore_signal(barrier, inc=1, device_id=(before, lax.rem(space + d, n_space)), device_id_type=MESH)

        @pl.when(d > 0)
        def _():
            pl.semaphore_signal(barrier, inc=1, device_id=(tm, lax.rem(space + d, n_space)), device_id_type=MESH)

        return carry

    lax.fori_loop(0, n_space, greet, 0)

    loads[0].wait()
    for f in range(FR):
        for h in range(TH):
            y[0, f, h * TW : (h + 1) * TW, :] = vid[f, h].astype(F32)
    pl.semaphore_wait(barrier, 2 * n_space - 1)

    row8 = lax.broadcasted_iota(jnp.int32, (8, C), 0)
    pending = []

    def send(t, k, source, target, device):
        copy = pltpu.make_async_remote_copy(
            src_ref=source,
            dst_ref=target,
            send_sem=send_sem.at[t, k],
            recv_sem=recv_sem.at[t, 0 if k < 4 else (1 if k < 8 else k - 6)],
            device_id=device,
            device_id_type=MESH,
        )
        copy.start()
        pending.append(copy)

    def arrived(t, k, buffer):
        pltpu.make_async_copy(buffer, buffer, recv_sem.at[t, k]).wait()

    def fill(slot, own, top, bottom, left_side, right_side):
        for c in range(3):
            off = PAD + 1 - c
            xc[slot, c, off : off + TW, :] = top
            xc[slot, c, off + TW : off + TW + CELLS, :] = own
            xc[slot, c, off + TW + CELLS : off + 2 * TW + CELLS, :] = bottom
        xc[slot, 0, pl.ds(PAD, TH + 2, stride=TW), :] = left_side
        xc[slot, 2, pl.ds(PAD + TW - 1, TH + 2, stride=TW), :] = right_side
        zeros = jnp.zeros((ROWS - CELLS, C), F32)
        for b in range(3):
            for c in range(3):
                start = PAD + b * TW
                part = jnp.concatenate([xc[slot, c, start : start + CELLS, :], zeros], axis=0)
                tap = b * 3 + c
                im[slot, :, tap * C : (tap + 1) * C] = part.astype(BF16)

    def side(column_part, top_corner, bottom_corner, keep):
        value = jnp.where(row8 == 0, top_corner, jnp.where(row8 == TH + 1, bottom_corner, column_part))
        return value, keep & ((row8 > 0) | (band > 0)) & ((row8 < TH + 1) | (band < BANDS - 1))

    def frame(slot, own, rims, corner_rows, act, keep):
        left_side, keep_left = side(rims[48:56], corner_rows[0], corner_rows[2], column > 0)
        right_side, keep_right = side(rims[56:64], corner_rows[1], corner_rows[3], column < TILE_COLS - 1)
        fill(
            slot,
            keep(act(own)),
            keep(jnp.where(band > 0, act(rims[4:24]), 0.0)),
            keep(jnp.where(band < BANDS - 1, act(rims[24:44]), 0.0)),
            keep(jnp.where(keep_left, act(left_side), 0.0)),
            keep(jnp.where(keep_right, act(right_side), 0.0)),
        )

    for t in range(LAYERS):
        s = t - 1
        if t > 0:
            value = y[t]
            sums = [jnp.sum(value[f], axis=0, keepdims=True) for f in range(FR)]
            squares = [jnp.sum(value[f] * value[f], axis=0, keepdims=True) for f in range(FR)]
            packed[s] = pack_sums(jnp.concatenate(sums + squares, axis=0))

            def tell(d, carry, s=s):
                pltpu.make_async_remote_copy(
                    src_ref=packed.at[s],
                    dst_ref=slots.at[s, d - 1],
                    send_sem=stat_send.at[s, 0],
                    recv_sem=stat_recv.at[s, 0],
                    device_id=(tm, lax.rem(space + d, n_space)),
                    device_id_type=MESH,
                ).start()
                return carry

            lax.fori_loop(1, n_space, tell, 0)

        for f in range(FR):
            cols[t, 0, f, 1 : TH + 1, :] = y[t, f, pl.ds(0, TH, stride=TW), :]
            cols[t, 1, f, 1 : TH + 1, :] = y[t, f, pl.ds(TW - 1, TH, stride=TW), :]
            for k, cell in enumerate((0, TW - 1, (TH - 1) * TW, CELLS - 1)):
                corners[t, k, f : f + 1, :] = y[t, f, cell : cell + 1, :]
        send(t, 0, y.at[t, :, 96:120], rim.at[t, :, 0:24], (tm, down * TILE_COLS + column))
        send(t, 1, y.at[t, :, 0:24], rim.at[t, :, 24:48], (tm, up * TILE_COLS + column))
        send(t, 2, cols.at[t, 1], rim.at[t, :, 48:56], (tm, band * TILE_COLS + right))
        send(t, 3, cols.at[t, 0], rim.at[t, :, 56:64], (tm, band * TILE_COLS + left))
        send(t, 4, corners.at[t, 0], rim_corner.at[t, 3], (tm, up * TILE_COLS + left))
        send(t, 5, corners.at[t, 1], rim_corner.at[t, 2], (tm, up * TILE_COLS + right))
        send(t, 6, corners.at[t, 2], rim_corner.at[t, 1], (tm, down * TILE_COLS + left))
        send(t, 7, corners.at[t, 3], rim_corner.at[t, 0], (tm, down * TILE_COLS + right))
        send(t, 8, y.at[t, 2:4], halo.at[t], (after, space))

        if t > 0:

            def tell_next(d, carry, s=s):
                pltpu.make_async_remote_copy(
                    src_ref=packed.at[s],
                    dst_ref=prev_slots.at[s, d],
                    send_sem=stat_send.at[s, 1],
                    recv_sem=stat_recv.at[s, 1],
                    device_id=(after, lax.rem(space + d, n_space)),
                    device_id_type=MESH,
                ).start()
                return carry

            lax.fori_loop(0, n_space, tell_next, 0)

        arrived(t, 0, rim.at[t])
        arrived(t, 1, rim_corner.at[t])
        send(t, 9, rim.at[t, 2:4], halo_rim.at[t], (after, space))
        send(t, 10, rim_corner.at[t], halo_corner.at[t], (after, space))

        if t == 0:
            loads[1].wait()

            def act_of(f, stats):
                return lambda value: value

            stats = None
        else:
            if t == 1:
                loads[4].wait()
                loads[5].wait()
            loads[1 + t].wait()
            gain = gains[s : s + 1, :]
            bias = biases[s : s + 1, :]

            def act_of(f, stats, bias=bias):
                mean, scale = stats

                def act(value):
                    v = (value - mean[f : f + 1]) * scale[f : f + 1] + bias
                    return v / (1.0 + jnp.exp(-v))

                return act

            pltpu.make_async_copy(slots.at[s], slots.at[s], stat_recv.at[s, 0]).wait()
            stats = moments(packed[s] + jnp.sum(slots[s], axis=0), gain)

        for f in range(FR):
            frame(
                2 + f,
                y[t, f, 0:CELLS, :],
                rim[t, f],
                [rim_corner[t, k, f : f + 1, :] for k in range(4)],
                act_of(f, stats),
                lambda value: value,
            )
        w21 = jnp.concatenate([w[t, 2], w[t, 1]], axis=1)
        two = dot(im[2:5].reshape(3 * ROWS, K), w21).reshape(3, ROWS, 2 * C)
        one = dot(im[5], w[t, 2])
        old = dot(im[2:4].reshape(2 * ROWS, K), w[t, 0]).reshape(2, ROWS, C)
        acc[0] = two[0, :, :C]
        acc[1] = two[0, :, C:] + two[1, :, :C]
        acc[2] = two[1, :, C:] + two[2, :, :C] + old[0]
        acc[3] = two[2, :, C:] + one + old[1]

        if t > 0:
            pltpu.make_async_copy(prev_slots.at[s], prev_slots.at[s], stat_recv.at[s, 1]).wait()
            stats = moments(jnp.sum(prev_slots[s], axis=0), gain)
        arrived(t, 2, halo.at[t])
        arrived(t, 3, halo_rim.at[t])
        arrived(t, 4, halo_corner.at[t])
        for f in range(2):
            frame(
                f,
                halo[t, f, 0:CELLS, :],
                halo_rim[t, f],
                [halo_corner[t, k, 2 + f : 3 + f, :] for k in range(4)],
                act_of(2 + f, stats),
                lambda value: jnp.where(tm > 0, value, 0.0),
            )
        w10 = jnp.concatenate([w[t, 1], w[t, 0]], axis=1)
        near = dot(im[1], w10)
        far = dot(im[0], w[t, 0])
        result = [acc[0] + near[:, :C] + far, acc[1] + near[:, C:], acc[2], acc[3]]
        for f in range(FR):
            if t < LAYERS - 1:
                y[t + 1, f] = result[f]
            else:
                for h in range(TH):
                    out[f, h] = result[f][h * TW : (h + 1) * TW].astype(BF16)

    for copy in pending:
        copy.wait_send()
    for s in range(LAYERS - 1):
        pltpu.make_async_copy(slots.at[s], slots.at[s], stat_send.at[s, 0]).wait()
        pltpu.make_async_copy(prev_slots.at[s], prev_slots.at[s], stat_send.at[s, 1]).wait()


def on_device(video, conv_weight, norm_gain, norm_bias):
    n_space = lax.axis_size("space")
    any_spec = pl.BlockSpec(memory_space=pl.ANY)
    result = pl.pallas_call(
        kernel,
        out_shape=jax.ShapeDtypeStruct((FR, TH, TW, C), BF16),
        in_specs=[any_spec] * 4,
        out_specs=pl.BlockSpec(memory_space=pltpu.VMEM),
        scratch_shapes=[
            pltpu.VMEM((LAYERS, 3, K, C), BF16),
            pltpu.VMEM((FR, TH, TW, C), BF16),
            pltpu.VMEM((LAYERS - 1, C), F32),
            pltpu.VMEM((LAYERS - 1, C), F32),
            pltpu.VMEM((LAYERS, FR, ROWS, C), F32),
            pltpu.VMEM((FR, ROWS, C), F32),
            pltpu.VMEM((FR + 2, 3, XROWS, C), F32),
            pltpu.VMEM((FR + 2, ROWS, K), BF16),
            pltpu.VMEM((LAYERS, 2, FR, 8, C), F32),
            pltpu.VMEM((LAYERS, 4, 8, C), F32),
            pltpu.VMEM((LAYERS, FR, 64, C), F32),
            pltpu.VMEM((LAYERS, 4, 8, C), F32),
            pltpu.VMEM((LAYERS, 2, ROWS, C), F32),
            pltpu.VMEM((LAYERS, 2, 64, C), F32),
            pltpu.VMEM((LAYERS, 4, 8, C), F32),
            pltpu.VMEM((LAYERS - 1, 2, C), F32),
            pltpu.VMEM((LAYERS - 1, n_space - 1, 2, C), F32),
            pltpu.VMEM((LAYERS - 1, n_space, 2, C), F32),
            pltpu.SemaphoreType.DMA((6,)),
            pltpu.SemaphoreType.DMA((LAYERS, 11)),
            pltpu.SemaphoreType.DMA((LAYERS, 5)),
            pltpu.SemaphoreType.DMA((LAYERS - 1, 2)),
            pltpu.SemaphoreType.DMA((LAYERS - 1, 2)),
        ],
        compiler_params=pltpu.CompilerParams(
            collective_id=0, has_side_effects=True, vmem_limit_bytes=48 << 20
        ),
        cost_estimate=pl.CostEstimate(flops=1274019840, bytes_accessed=2900000, transcendentals=300000),
        name="conv_stack",
    )(
        video.reshape(FR, TH, TW, C),
        conv_weight.reshape(LAYERS, 3, K, C),
        norm_gain,
        norm_bias,
    )
    return result[:, None]


def solution(mesh):
    placed = (P("tm", "space", None, None, None), P(), P(), P())
    return jax.shard_map(
        on_device,
        mesh=mesh,
        in_specs=placed,
        out_specs=P("tm", "space", None, None, None),
        check_vma=False,
    )
```

time: 426 us -> 43.9 us (0.10); the launches traced: 419 us -> 43.7 us
  blocking collectives: 232 us -> 0 us
  starting transfers between devices: 93 us -> 0 us
  Pallas kernels: 0 us -> 38.9 us
  local copies, waits for them, and re-layouts: 32 us -> 4.72 us
  other arithmetic: 22.9 us -> 0 us
  waiting for transfers between devices: 22.5 us -> 0 us
  matrix products: 15.2 us -> 0 us
    psum x4 -> x0, blocking collectives: 232 us -> none  [the longest x2 118 us: group_norm(): mean = lax.psum(group_sums(result, per), 'space') / count]
    ppermute x15 -> x0, starting transfers between devices: 93 us -> none  [shifted(): lax.ppermute(value, axis, [(source, source + steps) for source in range(l...]
    pallas_call x0 -> x1, Pallas kernels: none -> 38.9 us  [on_device(): pl.pallas_call(kernel, out_shape=jax.ShapeDtypeStruct((FR, TH, TW, C), BF...]
    ppermute x15 -> x0, waiting for transfers between devices: 22.5 us -> none  [shifted(): lax.ppermute(value, axis, [(source, source + steps) for source in range(l...]
    concatenate x33 -> x0, other arithmetic: 21.7 us -> none  [the longest x24 20.1 us: taps(): jnp.concatenate([block[step_t:step_t + frames, step_r:step_r + rows, step...]
    reshape x32 -> x0, local copies, waits for them, and re-layouts: 16.7 us -> none  [the longest x26 16.2 us: taps(): columns.reshape(-1, 3 * chans)]
    dot_general x27 -> x0, matrix products: 15.2 us -> none  [taps(): jnp.dot(columns.reshape(-1, 3 * chans), kernel[step_t, step_r], preferred...]
    slice x14 -> x0, local copies, waits for them, and re-layouts: 8.92 us -> none  [the longest x10 6.86 us: taps(): block[step_t:step_t + frames, step_r:step_r + rows, step_c:step_c + width]]
  transfers between devices with their start and end apart: 15 -> 0, of which waited for: 9 -> 0; matrix products, arithmetic and copies ran while one was open for 1% -> 0% of each run, Pallas kernels for 0% -> 0%
where the time goes in v1:
time: 43.9 us; the launch traced here: 43.7 us
  Pallas kernels  38.9 us (89%)
  local copies, waits for them, and re-layouts  4.72 us (11%)
    pallas_call x1, Pallas kernels, on_device(): pl.pallas_call(kernel, out_shape=jax.ShapeDtypeStruct((FR, TH, TW, C), BF...  38.9 us
    unnamed x7, local copies, waits for them, and re-layouts  4.03 us

profile of v1, /device:TPU:1, one launch (start us, length us, event | category | flops | bytes accessed | tf_op | source)
XLA Modules:
  0.0 43.7 jit_solution(14223028951648137869)
XLA Ops:
  0.0 0.9 %copy.8 = bf16[4,1,6,20,128]{4,3,2,0,1:T(8,128)(2,1)S(1)} copy(bf16[4,1,6,20,128]{4,0,3,2,1:T(4,128)(2,1)} %param.4) | data formatting | bytes 245760 | tf_op args[0]
  0.9 0.0 copy-start
  0.9 1.7 %copy-done = bf16[3,3,3,3,128,128]{5,4,3,2,1,0:T(8,128)(2,1)S(1)} copy-done((bf16[3,3,3,3,128,128]{5,4,3,2,1,0:T(8,128)(2,1)S(1)}, bf16[3,3,3,3,128,128]{5,4,3,2,1,0:T(8,128)(2,1)}, u32[]{:S(2)}) %copy-start) | copy-done | bytes 2654232
  2.7 0.0 copy-start.1
  2.7 0.7 %copy-done.1 = f32[2,128]{1,0:T(2,128)S(1)} copy-done((f32[2,128]{1,0:T(2,128)S(1)}, f32[2,128]{1,0:T(2,128)}, u32[]{:S(2)}) %copy-start.1) | copy-done | bytes 1048
  3.4 0.0 copy-start.2
  3.4 0.7 %copy-done.2 = f32[2,128]{1,0:T(2,128)S(1)} copy-done((f32[2,128]{1,0:T(2,128)S(1)}, f32[2,128]{1,0:T(2,128)}, u32[]{:S(2)}) %copy-start.2) | copy-done | bytes 1048
  4.0 38.9 %conv_stack.1 = bf16[4,6,20,128]{3,2,1,0:T(8,128)(2,1)S(1)} custom-call(bf16[4,6,20,128]{3,2,1,0:T(8,128)(2,1)S(1)} %bitcast.6, bf16[3,3,1152,128]{3,2,1,0:T(8,128)(2,1)S(1)} %bitcast.7, f32[2,128]{1,0:T(2,128)S(1)} %copy-done.1, f32[2,128]{1,0:T(2,128)S(1)} %copy-done.2), custom_call_target="tpu_custom_call" | custom-call | flops 1274019840 | bytes 2900000 | tf_op jit(solution)/shard_map/conv_stack/pallas_call | solution.py:322
  43.0 0.7 %copy.6 = bf16[4,1,6,20,128]{4,0,3,2,1:T(4,128)(2,1)} copy(bf16[4,1,6,20,128]{4,3,2,0,1:T(8,128)(2,1)S(1)} %bitcast.5) | data formatting | bytes 245760 | tf_op jit(solution)/shard_map/broadcast_in_dim | solution.py:363
Async XLA Ops:
  0.9 1.8 %copy-start = (bf16[3,3,3,3,128,128]{5,4,3,2,1,0:T(8,128)(2,1)S(1)}, bf16[3,3,3,3,128,128]{5,4,3,2,1,0:T(8,128)(2,1)}, u32[]{:S(2)}) copy-start(bf16[3,3,3,3,128,128]{5,4,3,2,1,0:T(8,128)(2,1)} %param.5) | copy-start | bytes 7962628
  2.7 0.7 %copy-start.1 = (f32[2,128]{1,0:T(2,128)S(1)}, f32[2,128]{1,0:T(2,128)}, u32[]{:S(2)}) copy-start(f32[2,128]{1,0:T(2,128)} %gain_in.1) | copy-start | bytes 3076
  3.4 0.7 %copy-start.2 = (f32[2,128]{1,0:T(2,128)S(1)}, f32[2,128]{1,0:T(2,128)}, u32[]{:S(2)}) copy-start(f32[2,128]{1,0:T(2,128)} %bias_in.1) | copy-start | bytes 3076

commit v2 on v1

v2 whole, which is shorter than its diff:
```python
import jax
import jax.numpy as jnp
from jax import lax
from jax.experimental import pallas as pl
from jax.experimental.pallas import tpu as pltpu
from jax.sharding import PartitionSpec as P

GROUPS = 32
TILE_COLS = 8
BANDS = 4
LAYERS = 3
EPS = 1e-05
F32 = jnp.float32
BF16 = jnp.bfloat16
MESH = pl.DeviceIdType.MESH

FR = 4
TH = 6
TW = 20
C = 128
CELLS = TH * TW
ROWS = 128
PAD = 8
XROWS = PAD + (TH + 2) * TW + 8
K = 9 * C
COUNT = BANDS * TH * TILE_COLS * TW * (C // GROUPS)


def dot(left, right):
    return jnp.dot(left, right, preferred_element_type=F32)


def pack_sums(total):
    lane = lax.broadcasted_iota(jnp.int32, (1, C), 1) % 4
    pair = total + pltpu.roll(total, 1, 1)
    quad = pair + pltpu.roll(pair, 2, 1)
    first = jnp.zeros((1, C), F32)
    second = jnp.zeros((1, C), F32)
    for f in range(FR):
        moved = quad if f == 3 else pltpu.roll(quad, C - (3 - f), 1)
        first = jnp.where(lane == f, moved[f : f + 1], first)
        second = jnp.where(lane == f, moved[4 + f : 5 + f], second)
    return jnp.concatenate([first, second], axis=0)


def unpack_sums(packed):
    lane = lax.broadcasted_iota(jnp.int32, (8, C), 1) % 4
    row = lax.broadcasted_iota(jnp.int32, (8, C), 0)
    spread = jnp.where(row < 4, packed[0:1], packed[1:2])
    only = jnp.where(lane == row % 4, spread, 0.0)
    lead = jnp.where(row % 4 == 0, only, 0.0)
    for f in range(1, FR):
        lead = jnp.where(row % 4 == f, pltpu.roll(only, C - f, 1), lead)
    pair = lead + pltpu.roll(lead, 1, 1)
    return pair + pltpu.roll(pair, 2, 1)


def moments(packed, gain):
    sums = unpack_sums(packed) * (1.0 / COUNT)
    mean = sums[0:4]
    var = sums[4:8] - mean * mean
    return mean, lax.rsqrt(var + EPS) * gain


def side(column_part, top_corner, bottom_corner):
    row = lax.broadcasted_iota(jnp.int32, (8, C), 0)
    return jnp.where(row == 0, top_corner, jnp.where(row == TH + 1, bottom_corner, column_part))


def far_first(i):
    k = i // 4
    return lax.rem(2 + 3 * lax.rem(i, 4), BANDS), lax.rem(4 + (k + 1) // 2 * (2 * lax.rem(k, 2) - 1), TILE_COLS)


SELF = 30

STEPS = ((1, 0), (-1, 0), (0, 1), (0, -1), (-1, -1), (-1, 1), (1, -1), (1, 1))
CORNERS = ((0, 0), (0, TW - 1), (TH - 1, 0), (TH - 1, TW - 1))


def kernel(
    video,
    weights,
    gain_in,
    bias_in,
    out,
    w,
    vid,
    inter,
    first_row,
    first_col,
    first_corner,
    row_cells,
    col_cells,
    gains,
    biases,
    y,
    acc,
    xc,
    im,
    stage_row,
    stage_col,
    stage_corner,
    out_row,
    out_col,
    out_corner,
    out_halo,
    in_row,
    in_col,
    in_corner,
    next_row,
    next_col,
    next_corner,
    halo,
    rim_row,
    rim_col,
    rim_corner,
    packed,
    slots,
    prev_slots,
    load_sem,
    send_sem,
    recv_sem,
    stat_send,
    stat_recv,
    near_sem,
    ready_sem,
):
    tm = lax.axis_index("tm")
    space = lax.axis_index("space")
    n_tm = lax.axis_size("tm")
    n_space = lax.axis_size("space")
    band = space // TILE_COLS
    column = lax.rem(space, TILE_COLS)
    after = lax.rem(tm + 1, n_tm)
    before = lax.rem(tm + n_tm - 1, n_tm)

    def tile(bands, columns):
        return lax.rem(band + bands + BANDS, BANDS) * TILE_COLS + lax.rem(column + columns + TILE_COLS, TILE_COLS)

    barrier = pltpu.get_barrier_semaphore()
    for step in STEPS:
        pl.semaphore_signal(barrier, inc=1, device_id=(tm, tile(*step)), device_id_type=MESH)
    for step in ((0, 0),) + STEPS:
        pl.semaphore_signal(barrier, inc=1, device_id=(before, tile(*step)), device_id_type=MESH)

    loads = [pltpu.make_async_copy(video, vid, load_sem.at[0])]
    for layer in range(LAYERS):
        loads.append(pltpu.make_async_copy(weights.at[layer], w.at[layer], load_sem.at[1 + layer]))
    loads.append(pltpu.make_async_copy(gain_in, gains, load_sem.at[4]))
    loads.append(pltpu.make_async_copy(bias_in, biases, load_sem.at[5]))
    for copy in loads:
        copy.start()
    loads[0].wait()
    inter[...] = vid[...].astype(F32).reshape(FR * CELLS, C)
    for f in range(2):
        whole = jnp.concatenate([inter[pl.ds(2 + f, CELLS, stride=FR), :], jnp.zeros((ROWS - CELLS, C), F32)], axis=0)
        out_halo[0, f] = whole.astype(BF16)
    pl.semaphore_wait(barrier, 2 * len(STEPS) + 1)

    sent = {}

    def send(t, k, source, target, device):
        copy = pltpu.make_async_remote_copy(
            src_ref=source,
            dst_ref=target,
            send_sem=send_sem.at[t, k],
            recv_sem=recv_sem.at[t, k],
            device_id=device,
            device_id_type=MESH,
        )
        copy.start()
        sent[t, k] = copy

    def fill(slot, own, top, bottom, left_side, right_side):
        for c in range(3):
            off = PAD + 1 - c
            xc[slot, c, off : off + TW, :] = top
            xc[slot, c, off + TW : off + TW + CELLS, :] = own
            xc[slot, c, off + TW + CELLS : off + 2 * TW + CELLS, :] = bottom
        xc[slot, 0, pl.ds(PAD, TH + 2, stride=TW), :] = left_side
        xc[slot, 2, pl.ds(PAD + TW - 1, TH + 2, stride=TW), :] = right_side
        zeros = jnp.zeros((ROWS - CELLS, C), F32)
        for b in range(3):
            for c in range(3):
                start = PAD + b * TW
                part = jnp.concatenate([xc[slot, c, start : start + CELLS, :], zeros], axis=0)
                tap = b * 3 + c
                im[slot, :, tap * C : (tap + 1) * C] = part.astype(BF16)

    row8 = lax.broadcasted_iota(jnp.int32, (8, C), 0)
    keep_rows = ((row8 > 0) | (band > 0)) & ((row8 < TH + 1) | (band < BANDS - 1))
    keep_left = keep_rows & (column > 0)
    keep_right = keep_rows & (column < TILE_COLS - 1)

    def frame(slot, parts, act, keep):
        own, top, bottom, left_side, right_side = (act(*part) for part in parts)
        fill(
            slot,
            keep(own),
            keep(jnp.where(band > 0, top, 0.0)),
            keep(jnp.where(band < BANDS - 1, bottom, 0.0)),
            keep(jnp.where(keep_left, left_side, 0.0)),
            keep(jnp.where(keep_right, right_side, 0.0)),
        )

    def same(value, shift=None):
        return value

    def later(value):
        return jnp.where(tm > 0, value, 0.0)

    def split(g, f):
        return (
            (row_cells[g, 0, pl.ds(f, TW, stride=FR), :], None),
            (row_cells[g, 1, pl.ds(f, TW, stride=FR), :], None),
            (col_cells[g, 0, pl.ds(f, TH + 2, stride=FR), :], None),
            (col_cells[g, 1, pl.ds(f, TH + 2, stride=FR), :], None),
        )

    def unpack_rims(g):
        for i in range(2):
            row_cells[g, i] = first_row[g, i].astype(F32).reshape(FR * TW, C)
            col_cells[g, i, FR : FR * (TH + 1), :] = first_col[g, i].astype(F32).reshape(FR * TH, C)
            col_cells[g, i, 0:FR, :] = first_corner[g, i].astype(F32).reshape(FR, C)
            col_cells[g, i, FR * (TH + 1) :, :] = first_corner[g, 2 + i].astype(F32).reshape(FR, C)

    def rims_of(p, f):
        lo = f * TW
        own = 2 * p + f
        rims = [(rim_row[i, p, lo : lo + TW, :], rim_row[i, p, 2 * TW + f : 2 * TW + f + 1, :]) for i in range(2)]
        for i in range(2):
            part = rim_col[i, p, 8 * f : 8 * f + 8, :]
            upper, lower = ((rim_corner[k, 0, own : own + 1, :], rim_corner[k, 1, own : own + 1, :]) for k in (i, 2 + i))
            rims.append((side(part, upper[0], lower[0]), side(part[0:1], upper[1], lower[1])))
        return rims

    for t in range(LAYERS):
        s = t - 1
        if t == 0:
            rims = [vid.at[TH - 1], vid.at[0], vid.at[:, TW - 1], vid.at[:, 0]] + [vid.at[h, pl.ds(c, 1)] for h, c in CORNERS]
            for g, where_to in ((0, tm), (1, after)):
                lands = [first_row.at[g, 0], first_row.at[g, 1], first_col.at[g, 0], first_col.at[g, 1]] + [
                    first_corner.at[g, 3 - k] for k in range(4)
                ]
                for k, step in enumerate(STEPS):
                    send(0, 9 * g + k, rims[k], lands[k], (where_to, tile(*step)))
                if g == 0:
                    send(0, 8, out_halo.at[0], halo.at[0], (after, space))
        else:
            value = y[s]
            sums = [jnp.sum(value[f], axis=0, keepdims=True) for f in range(FR)]
            squares = [jnp.sum(value[f] * value[f], axis=0, keepdims=True) for f in range(FR)]
            packed[s] = pack_sums(jnp.concatenate(sums + squares, axis=0))

            def tell(i, slot, s=s):
                pltpu.make_async_remote_copy(
                    src_ref=packed.at[s],
                    dst_ref=slots.at[s, slot],
                    send_sem=stat_send.at[s, 0],
                    recv_sem=stat_recv.at[s, 0],
                    device_id=(tm, tile(*far_first(i))),
                    device_id_type=MESH,
                ).start()

            def tell_next(i, carry, s=s):
                pltpu.make_async_remote_copy(
                    src_ref=packed.at[s],
                    dst_ref=prev_slots.at[s, i],
                    send_sem=stat_send.at[s, 1],
                    recv_sem=stat_recv.at[s, 1],
                    device_id=(after, tile(*far_first(i))),
                    device_id_type=MESH,
                ).start()
                return carry

            def tell_one(i, carry, tell=tell):
                tell(i, i)
                return carry

            lax.fori_loop(0, SELF, tell_one, 0)
            tell(SELF + 1, SELF)
            if t == 1:
                pl.semaphore_wait(ready_sem, 1)
            lax.fori_loop(0, n_space, tell_next, 0)

            for f in range(FR):
                off = (sums[f] * (1.0 / CELLS)).astype(BF16).astype(F32)
                p, lo = f // 2, f % 2
                for i, first in enumerate((CELLS - TW, 0)):
                    stage_row[i, p, lo * TW : (lo + 1) * TW, :] = y[s, f, first : first + TW, :] - off
                    stage_row[i, p, 2 * TW + lo : 2 * TW + lo + 1, :] = off
                for i, first in enumerate((TW - 1, 0)):
                    stage_col[i, p, 8 * lo : 8 * lo + 8, :] = jnp.broadcast_to(off, (8, C))
                    stage_col[i, p, 8 * lo + 1 : 8 * lo + 1 + TH, :] = y[s, f, pl.ds(first, TH, stride=TW), :] - off
                for k, (h, c) in enumerate(CORNERS):
                    cell = h * TW + c
                    stage_corner[k, 0, f : f + 1, :] = y[s, f, cell : cell + 1, :] - off
                    stage_corner[k, 1, f : f + 1, :] = off
                if p == 1:
                    whole = jnp.concatenate([y[s, f, 0:CELLS, :] - off, jnp.broadcast_to(off, (ROWS - CELLS, C))], axis=0)
                    out_halo[t, lo] = whole.astype(BF16)
            out_row[s] = stage_row[...].astype(BF16)
            out_col[s] = stage_col[...].astype(BF16)
            out_corner[s] = stage_corner[...].astype(BF16)
            for k, step in enumerate(STEPS):
                if k < 2:
                    source, land = out_row.at[s, k], in_row.at[s, k]
                elif k < 4:
                    source, land = out_col.at[s, k - 2], in_col.at[s, k - 2]
                else:
                    source, land = out_corner.at[s, k - 4], in_corner.at[s, 7 - k]
                send(t, k, source, land, (tm, tile(*step)))
            send(t, 8, out_halo.at[t], halo.at[t], (after, space))
            for k, step in enumerate(STEPS):
                if k < 2:
                    source, land = out_row.at[s, k, 1], next_row.at[s, k]
                elif k < 4:
                    source, land = out_col.at[s, k - 2, 1], next_col.at[s, k - 2]
                else:
                    source, land = out_corner.at[s, k - 4], next_corner.at[s, 7 - k]
                send(t, 9 + k, source, land, (after, tile(*step)))

        for k in range(8):
            sent[t, k].wait_recv()
        loads[1 + t].wait()

        if t == 0:
            for columns in (2, -2):
                pl.semaphore_signal(near_sem, inc=1, device_id=(tm, tile(0, columns)), device_id_type=MESH)
            unpack_rims(0)
            for f in range(FR):
                frame(2 + f, [(inter[pl.ds(f, CELLS, stride=FR), :], None), *split(0, f)], same, same)
        else:
            if t == 1:
                loads[4].wait()
                loads[5].wait()
            gain = gains[s : s + 1, :]
            bias = biases[s : s + 1, :]

            def act_of(f, stats, bias=bias):
                mean, scale = stats

                def act(value, off=0.0):
                    v = (value + (off - mean[f : f + 1])) * scale[f : f + 1] + bias
                    return v / (1.0 + jnp.exp(-v))

                return act

            rim_row[...] = in_row[s].astype(F32)
            rim_col[...] = in_col[s].astype(F32)
            rim_corner[...] = in_corner[s].astype(F32)
            pltpu.make_async_copy(slots.at[s], slots.at[s], stat_recv.at[s, 0]).wait()
            stats = moments(packed[s] + jnp.sum(slots[s], axis=0), gain)
            for f in range(FR):
                frame(2 + f, [(y[s, f, 0:CELLS, :],), *rims_of(f // 2, f % 2)], act_of(f, stats), same)

        w21 = jnp.concatenate([w[t, 2], w[t, 1]], axis=1)
        two = dot(im[2:5].reshape(3 * ROWS, K), w21).reshape(3, ROWS, 2 * C)
        one = dot(im[5], w[t, 2])
        old = dot(im[2:4].reshape(2 * ROWS, K), w[t, 0]).reshape(2, ROWS, C)
        acc[0] = two[0, :, :C]
        acc[1] = two[0, :, C:] + two[1, :, :C]
        acc[2] = two[1, :, C:] + two[2, :, :C] + old[0]
        acc[3] = two[2, :, C:] + one + old[1]

        for k in range(8, 17):
            sent[t, k].wait_recv()
        if t == 0:
            pl.semaphore_wait(near_sem, 2)
            pl.semaphore_signal(ready_sem, inc=1, device_id=(before, space), device_id_type=MESH)
            unpack_rims(1)
            for f in range(2):
                frame(f, [(halo[0, f].astype(F32)[0:CELLS],), *split(1, 2 + f)], same, later)
        else:
            for i in range(2):
                rim_row[i, 1] = next_row[s, i].astype(F32)
                rim_col[i, 1] = next_col[s, i].astype(F32)
            rim_corner[...] = next_corner[s].astype(F32)
            pltpu.make_async_copy(prev_slots.at[s], prev_slots.at[s], stat_recv.at[s, 1]).wait()
            stats = moments(jnp.sum(prev_slots[s], axis=0), gain)
            for f in range(2):
                whole = halo[t, f].astype(F32)
                frame(f, [(whole[0:CELLS], whole[CELLS : CELLS + 1]), *rims_of(1, f)], act_of(2 + f, stats), later)
        w10 = jnp.concatenate([w[t, 1], w[t, 0]], axis=1)
        near = dot(im[1], w10)
        far = dot(im[0], w[t, 0])
        result = [acc[0] + near[:, :C] + far, acc[1] + near[:, C:], acc[2], acc[3]]
        for f in range(FR):
            if t < LAYERS - 1:
                y[t, f] = result[f]
            else:
                for h in range(TH):
                    out[f, h] = result[f][h * TW : (h + 1) * TW].astype(BF16)

    for copy in sent.values():
        copy.wait_send()
    for s in range(LAYERS - 1):
        pltpu.make_async_copy(slots.at[s], slots.at[s], stat_send.at[s, 0]).wait()
        pltpu.make_async_copy(prev_slots.at[s], prev_slots.at[s], stat_send.at[s, 1]).wait()


def on_device(video, conv_weight, norm_gain, norm_bias):
    n_space = lax.axis_size("space")
    inner = LAYERS - 1
    arguments = (
        video.reshape(FR, TH, TW, C).transpose(1, 2, 0, 3),
        conv_weight.reshape(LAYERS, 3, K, C),
        norm_gain,
        norm_bias,
    )
    result = pl.pallas_call(
        kernel,
        out_shape=jax.ShapeDtypeStruct((FR, TH, TW, C), BF16),
        in_specs=[pl.BlockSpec(memory_space=pltpu.HBM)] * 4,
        out_specs=pl.BlockSpec(memory_space=pltpu.VMEM),
        scratch_shapes=[
            pltpu.VMEM((LAYERS, 3, K, C), BF16),
            pltpu.VMEM((TH, TW, FR, C), BF16),
            pltpu.VMEM((FR * CELLS, C), F32),
            pltpu.VMEM((2, 2, TW, FR, C), BF16),
            pltpu.VMEM((2, 2, TH, FR, C), BF16),
            pltpu.VMEM((2, 4, 1, FR, C), BF16),
            pltpu.VMEM((2, 2, FR * TW, C), F32),
            pltpu.VMEM((2, 2, FR * (TH + 2), C), F32),
            pltpu.VMEM((inner, C), F32),
            pltpu.VMEM((inner, C), F32),
            pltpu.VMEM((inner, FR, ROWS, C), F32),
            pltpu.VMEM((FR, ROWS, C), F32),
            pltpu.VMEM((FR + 2, 3, XROWS, C), F32),
            pltpu.VMEM((FR + 2, ROWS, K), BF16),
            pltpu.VMEM((2, 2, 48, C), F32),
            pltpu.VMEM((2, 2, 16, C), F32),
            pltpu.VMEM((4, 2, FR, C), F32),
            pltpu.VMEM((inner, 2, 2, 48, C), BF16),
            pltpu.VMEM((inner, 2, 2, 16, C), BF16),
            pltpu.VMEM((inner, 4, 2, FR, C), BF16),
            pltpu.VMEM((LAYERS, 2, ROWS, C), BF16),
            pltpu.VMEM((inner, 2, 2, 48, C), BF16),
            pltpu.VMEM((inner, 2, 2, 16, C), BF16),
            pltpu.VMEM((inner, 4, 2, FR, C), BF16),
            pltpu.VMEM((inner, 2, 48, C), BF16),
            pltpu.VMEM((inner, 2, 16, C), BF16),
            pltpu.VMEM((inner, 4, 2, FR, C), BF16),
            pltpu.VMEM((LAYERS, 2, ROWS, C), BF16),
            pltpu.VMEM((2, 2, 48, C), F32),
            pltpu.VMEM((2, 2, 16, C), F32),
            pltpu.VMEM((4, 2, FR, C), F32),
            pltpu.VMEM((inner, 2, C), F32),
            pltpu.VMEM((inner, n_space - 1, 2, C), F32),
            pltpu.VMEM((inner, n_space, 2, C), F32),
            pltpu.SemaphoreType.DMA((6,)),
            pltpu.SemaphoreType.DMA((LAYERS, 17)),
            pltpu.SemaphoreType.DMA((LAYERS, 17)),
            pltpu.SemaphoreType.DMA((inner, 2)),
            pltpu.SemaphoreType.DMA((inner, 2)),
            pltpu.SemaphoreType.REGULAR,
            pltpu.SemaphoreType.REGULAR,
        ],
        compiler_params=pltpu.CompilerParams(collective_id=0, has_side_effects=True, vmem_limit_bytes=48 << 20),
        cost_estimate=pl.CostEstimate(flops=1274019840, bytes_accessed=2900000, transcendentals=300000),
        name="conv_stack",
    )(*(pltpu.with_memory_space_constraint(value, pltpu.HBM) for value in arguments))
    return result[:, None]


def solution(mesh):
    placed = (P("tm", "space", None, None, None), P(), P(), P())
    return jax.shard_map(
        on_device,
        mesh=mesh,
        in_specs=placed,
        out_specs=P("tm", "space", None, None, None),
        check_vma=False,
    )
```

time: 43.9 us -> 37.3 us (0.85)
  local copies, waits for them, and re-layouts: 4.72 us -> 0.7 us
  Pallas kernels: 38.9 us -> 36.4 us
    unnamed x7 -> x0, local copies, waits for them, and re-layouts: 4.03 us -> none
    pallas_call x1, Pallas kernels: 38.9 us -> 36.4 us  [on_device(): pl.pallas_call(kernel, out_shape=jax.ShapeDtypeStruct((FR, TH, TW, C), BF...]
where the time goes in v2:
time: 37.3 us; the launch traced here: 37.1 us
  Pallas kernels  36.4 us (98%)
  local copies, waits for them, and re-layouts  0.7 us (2%)
    pallas_call x1, Pallas kernels, on_device(): pl.pallas_call(kernel, out_shape=jax.ShapeDtypeStruct((FR, TH, TW, C), BF...  36.4 us

profile of v2, /device:TPU:1, one launch (start us, length us, event | category | flops | bytes accessed | tf_op | source)
XLA Modules:
  0.0 37.1 jit_solution(590858469669072313)
XLA Ops:
  0.0 36.4 %conv_stack.1 = bf16[4,6,20,128]{3,2,1,0:T(8,128)(2,1)S(1)} custom-call(bf16[6,20,4,128]{3,2,1,0:T(4,128)(2,1)} %bitcast.7, bf16[3,3,1152,128]{3,2,1,0:T(8,128)(2,1)} %bitcast.6, f32[2,128]{1,0:T(2,128)} %gain_in.1, f32[2,128]{1,0:T(2,128)} %bias_in.1), custom_call_target="tpu_custom_call" | custom-call | flops 1274019840 | bytes 2900000 | tf_op jit(solution)/shard_map/conv_stack/pallas_call | solution.py:412
  36.4 0.7 %copy.5 = bf16[4,1,6,20,128]{4,0,3,2,1:T(4,128)(2,1)} copy(bf16[4,1,6,20,128]{4,3,2,0,1:T(8,128)(2,1)S(1)} %bitcast.5) | data formatting | bytes 245760 | tf_op jit(solution)/shard_map/broadcast_in_dim | solution.py:464

commit v3 on v2

--- a/solution.py
+++ b/solution.py
@@ -30,16 +30,19 @@
     return jnp.dot(left, right, preferred_element_type=F32)
 
 
+def roll(value, steps):
+    return value if steps == 0 else pltpu.roll(value, steps % C, 1)
+
+
 def pack_sums(total):
     lane = lax.broadcasted_iota(jnp.int32, (1, C), 1) % 4
-    pair = total + pltpu.roll(total, 1, 1)
-    quad = pair + pltpu.roll(pair, 2, 1)
+    moved = {d: roll(total, d) for d in range(-3, 4)}
     first = jnp.zeros((1, C), F32)
     second = jnp.zeros((1, C), F32)
     for f in range(FR):
-        moved = quad if f == 3 else pltpu.roll(quad, C - (3 - f), 1)
-        first = jnp.where(lane == f, moved[f : f + 1], first)
-        second = jnp.where(lane == f, moved[4 + f : 5 + f], second)
+        group = (moved[f - 3] + moved[f - 2]) + (moved[f - 1] + moved[f])
+        first = jnp.where(lane == f, group[f : f + 1], first)
+        second = jnp.where(lane == f, group[4 + f : 5 + f], second)
     return jnp.concatenate([first, second], axis=0)
 
 
@@ -47,12 +50,11 @@
     lane = lax.broadcasted_iota(jnp.int32, (8, C), 1) % 4
     row = lax.broadcasted_iota(jnp.int32, (8, C), 0)
     spread = jnp.where(row < 4, packed[0:1], packed[1:2])
-    only = jnp.where(lane == row % 4, spread, 0.0)
-    lead = jnp.where(row % 4 == 0, only, 0.0)
-    for f in range(1, FR):
-        lead = jnp.where(row % 4 == f, pltpu.roll(only, C - f, 1), lead)
-    pair = lead + pltpu.roll(lead, 1, 1)
-    return pair + pltpu.roll(pair, 2, 1)
+    gap = lane - row % 4
+    result = spread
+    for d in (-3, -2, -1, 1, 2, 3):
+        result = jnp.where(gap == d, roll(spread, d), result)
+    return result
 
 
 def moments(packed, gain):
@@ -67,12 +69,9 @@
     return jnp.where(row == 0, top_corner, jnp.where(row == TH + 1, bottom_corner, column_part))
 
 
-def far_first(i):
-    k = i // 4
-    return lax.rem(2 + 3 * lax.rem(i, 4), BANDS), lax.rem(4 + (k + 1) // 2 * (2 * lax.rem(k, 2) - 1), TILE_COLS)
-
-
-SELF = 30
+FAR_FIRST = sorted(
+    ((b, c) for b in range(-1, 3) for c in range(-3, 5) if (b, c) != (0, 0)), key=lambda o: (-abs(o[0]) - abs(o[1]), o)
+)
 
 STEPS = ((1, 0), (-1, 0), (0, 1), (0, -1), (-1, -1), (-1, 1), (1, -1), (1, 1))
 CORNERS = ((0, 0), (0, TW - 1), (TH - 1, 0), (TH - 1, TW - 1))
@@ -135,14 +134,23 @@
     after = lax.rem(tm + 1, n_tm)
     before = lax.rem(tm + n_tm - 1, n_tm)
 
-    def tile(bands, columns):
-        return lax.rem(band + bands + BANDS, BANDS) * TILE_COLS + lax.rem(column + columns + TILE_COLS, TILE_COLS)
+    bands = {b: lax.rem(band + b + BANDS, BANDS) * TILE_COLS for b in range(-1, 3)}
+    columns = {c: lax.rem(column + c + TILE_COLS, TILE_COLS) for c in range(-3, 5)}
+    tiles = {(b, c): bands[b] + columns[c] for b in bands for c in columns}
+
+    def tile(b, c):
+        return tiles[b, c]
 
     barrier = pltpu.get_barrier_semaphore()
-    for step in STEPS:
+    has_before = has_after = True
+
+    @pl.when(has_before)
+    def _():
+        for step in STEPS[::-1] + ((0, 0),):
+            pl.semaphore_signal(barrier, inc=1, device_id=(before, tile(*step)), device_id_type=MESH)
+
+    for step in STEPS[::-1]:
         pl.semaphore_signal(barrier, inc=1, device_id=(tm, tile(*step)), device_id_type=MESH)
-    for step in ((0, 0),) + STEPS:
-        pl.semaphore_signal(barrier, inc=1, device_id=(before, tile(*step)), device_id_type=MESH)
 
     loads = [pltpu.make_async_copy(video, vid, load_sem.at[0])]
     for layer in range(LAYERS):
@@ -239,50 +247,46 @@
         s = t - 1
         if t == 0:
             rims = [vid.at[TH - 1], vid.at[0], vid.at[:, TW - 1], vid.at[:, 0]] + [vid.at[h, pl.ds(c, 1)] for h, c in CORNERS]
-            for g, where_to in ((0, tm), (1, after)):
+
+            def give(g, where_to, rims=rims):
                 lands = [first_row.at[g, 0], first_row.at[g, 1], first_col.at[g, 0], first_col.at[g, 1]] + [
                     first_corner.at[g, 3 - k] for k in range(4)
                 ]
-                for k, step in enumerate(STEPS):
-                    send(0, 9 * g + k, rims[k], lands[k], (where_to, tile(*step)))
-                if g == 0:
-                    send(0, 8, out_halo.at[0], halo.at[0], (after, space))
+                for k in range(7, -1, -1):
+                    send(0, 9 * g + k, rims[k], lands[k], (where_to, tile(*STEPS[k])))
+
+            give(0, tm)
+
+            @pl.when(has_after)
+            def _(give=give):
+                send(0, 8, out_halo.at[0], halo.at[0], (after, space))
+                give(1, after)
+
         else:
             value = y[s]
             sums = [jnp.sum(value[f], axis=0, keepdims=True) for f in range(FR)]
             squares = [jnp.sum(value[f] * value[f], axis=0, keepdims=True) for f in range(FR)]
             packed[s] = pack_sums(jnp.concatenate(sums + squares, axis=0))
 
-            def tell(i, slot, s=s):
+            def tell(k, offset, device, buffer, mine, s=s):
                 pltpu.make_async_remote_copy(
                     src_ref=packed.at[s],
-                    dst_ref=slots.at[s, slot],
-                    send_sem=stat_send.at[s, 0],
-                    recv_sem=stat_recv.at[s, 0],
-                    device_id=(tm, tile(*far_first(i))),
+                    dst_ref=buffer.at[s, k],
+                    send_sem=stat_send.at[s, mine],
+                    recv_sem=stat_recv.at[s, mine],
+                    device_id=(device, tile(*offset)),
                     device_id_type=MESH,
                 ).start()
 
-            def tell_next(i, carry, s=s):
-                pltpu.make_async_remote_copy(
-                    src_ref=packed.at[s],
-                    dst_ref=prev_slots.at[s, i],
-                    send_sem=stat_send.at[s, 1],
-                    recv_sem=stat_recv.at[s, 1],
-                    device_id=(after, tile(*far_first(i))),
-                    device_id_type=MESH,
-                ).start()
-                return carry
-
-            def tell_one(i, carry, tell=tell):
-                tell(i, i)
-                return carry
-
-            lax.fori_loop(0, SELF, tell_one, 0)
-            tell(SELF + 1, SELF)
-            if t == 1:
-                pl.semaphore_wait(ready_sem, 1)
-            lax.fori_loop(0, n_space, tell_next, 0)
+            for k, offset in enumerate(FAR_FIRST):
+                tell(k, offset, tm, slots, 0)
+
+            @pl.when(has_after)
+            def _(tell=tell, t=t):
+                if t == 1:
+                    pl.semaphore_wait(ready_sem, 1)
+                for k, offset in enumerate(FAR_FIRST + [(0, 0)]):
+                    tell(k, offset, after, prev_slots, 1)
 
             for f in range(FR):
                 off = (sums[f] * (1.0 / CELLS)).astype(BF16).astype(F32)
@@ -303,31 +307,34 @@
             out_row[s] = stage_row[...].astype(BF16)
             out_col[s] = stage_col[...].astype(BF16)
             out_corner[s] = stage_corner[...].astype(BF16)
-            for k, step in enumerate(STEPS):
+            for k in range(7, -1, -1):
                 if k < 2:
                     source, land = out_row.at[s, k], in_row.at[s, k]
                 elif k < 4:
                     source, land = out_col.at[s, k - 2], in_col.at[s, k - 2]
                 else:
                     source, land = out_corner.at[s, k - 4], in_corner.at[s, 7 - k]
-                send(t, k, source, land, (tm, tile(*step)))
-            send(t, 8, out_halo.at[t], halo.at[t], (after, space))
-            for k, step in enumerate(STEPS):
-                if k < 2:
-                    source, land = out_row.at[s, k, 1], next_row.at[s, k]
-                elif k < 4:
-                    source, land = out_col.at[s, k - 2, 1], next_col.at[s, k - 2]
-                else:
-                    source, land = out_corner.at[s, k - 4], next_corner.at[s, 7 - k]
-                send(t, 9 + k, source, land, (after, tile(*step)))
+                send(t, k, source, land, (tm, tile(*STEPS[k])))
+
+            @pl.when(has_after)
+            def _(s=s, t=t):
+                send(t, 8, out_halo.at[t], halo.at[t], (after, space))
+                for k in range(7, -1, -1):
+                    if k < 2:
+                        source, land = out_row.at[s, k, 1], next_row.at[s, k]
+                    elif k < 4:
+                        source, land = out_col.at[s, k - 2, 1], next_col.at[s, k - 2]
+                    else:
+                        source, land = out_corner.at[s, k - 4], next_corner.at[s, 7 - k]
+                    send(t, 9 + k, source, land, (after, tile(*STEPS[k])))
 
         for k in range(8):
             sent[t, k].wait_recv()
         loads[1 + t].wait()
 
         if t == 0:
-            for columns in (2, -2):
-                pl.semaphore_signal(near_sem, inc=1, device_id=(tm, tile(0, columns)), device_id_type=MESH)
+            for step in ((0, 2), (0, -2)):
+                pl.semaphore_signal(near_sem, inc=1, device_id=(tm, tile(*step)), device_id_type=MESH)
             unpack_rims(0)
             for f in range(FR):
                 frame(2 + f, [(inter[pl.ds(f, CELLS, stride=FR), :], None), *split(0, f)], same, same)
@@ -364,11 +371,19 @@
         acc[2] = two[1, :, C:] + two[2, :, :C] + old[0]
         acc[3] = two[2, :, C:] + one + old[1]
 
-        for k in range(8, 17):
-            sent[t, k].wait_recv()
         if t == 0:
             pl.semaphore_wait(near_sem, 2)
-            pl.semaphore_signal(ready_sem, inc=1, device_id=(before, space), device_id_type=MESH)
+
+        @pl.when(has_before)
+        def _(s=s, t=t):
+            for k in range(8, 17):
+                sent[t, k].wait_recv()
+            if t == 0:
+                pl.semaphore_signal(ready_sem, inc=1, device_id=(before, space), device_id_type=MESH)
+            else:
+                pltpu.make_async_copy(prev_slots.at[s], prev_slots.at[s], stat_recv.at[s, 1]).wait()
+
+        if t == 0:
             unpack_rims(1)
             for f in range(2):
                 frame(f, [(halo[0, f].astype(F32)[0:CELLS],), *split(1, 2 + f)], same, later)
@@ -377,7 +392,6 @@
                 rim_row[i, 1] = next_row[s, i].astype(F32)
                 rim_col[i, 1] = next_col[s, i].astype(F32)
             rim_corner[...] = next_corner[s].astype(F32)
-            pltpu.make_async_copy(prev_slots.at[s], prev_slots.at[s], stat_recv.at[s, 1]).wait()
             stats = moments(jnp.sum(prev_slots[s], axis=0), gain)
             for f in range(2):
                 whole = halo[t, f].astype(F32)
@@ -393,11 +407,19 @@
                 for h in range(TH):
                     out[f, h] = result[f][h * TW : (h + 1) * TW].astype(BF16)
 
-    for copy in sent.values():
-        copy.wait_send()
+    for t in range(LAYERS):
+        for k in range(8):
+            sent[t, k].wait_send()
     for s in range(LAYERS - 1):
         pltpu.make_async_copy(slots.at[s], slots.at[s], stat_send.at[s, 0]).wait()
-        pltpu.make_async_copy(prev_slots.at[s], prev_slots.at[s], stat_send.at[s, 1]).wait()
+
+    @pl.when(has_after)
+    def _():
+        for t in range(LAYERS):
+            for k in range(8, 17):
+                sent[t, k].wait_send()
+        for s in range(LAYERS - 1):
+            pltpu.make_async_copy(prev_slots.at[s], prev_slots.at[s], stat_send.at[s, 1]).wait()
 
 
 def on_device(video, conv_weight, norm_gain, norm_bias):

time: 37.3 us -> 35.9 us (0.962)
  Pallas kernels: 36.4 us -> 35 us
    pallas_call x1, Pallas kernels: 36.4 us -> 35 us  [on_device(): pl.pallas_call(kernel, out_shape=jax.ShapeDtypeStruct((FR, TH, TW, C), BF...]
where the time goes in v3:
time: 35.9 us; the launch traced here: 35.7 us
  Pallas kernels  35 us (97%)
  local copies, waits for them, and re-layouts  0.7 us (2%)
    pallas_call x1, Pallas kernels, on_device(): pl.pallas_call(kernel, out_shape=jax.ShapeDtypeStruct((FR, TH, TW, C), BF...  35 us

profile of v3, /device:TPU:1, one launch (start us, length us, event | category | flops | bytes accessed | tf_op | source)
XLA Modules:
  0.0 35.7 jit_solution(1670051107413006045)
XLA Ops:
  0.0 35.0 %conv_stack.1 = bf16[4,6,20,128]{3,2,1,0:T(8,128)(2,1)S(1)} custom-call(bf16[6,20,4,128]{3,2,1,0:T(4,128)(2,1)} %bitcast.7, bf16[3,3,1152,128]{3,2,1,0:T(8,128)(2,1)} %bitcast.6, f32[2,128]{1,0:T(2,128)} %gain_in.1, f32[2,128]{1,0:T(2,128)} %bias_in.1), custom_call_target="tpu_custom_call" | custom-call | flops 1274019840 | bytes 2900000 | tf_op jit(solution)/shard_map/conv_stack/pallas_call | solution.py:434
  35.0 0.7 %copy.5 = bf16[4,1,6,20,128]{4,0,3,2,1:T(4,128)(2,1)} copy(bf16[4,1,6,20,128]{4,3,2,0,1:T(8,128)(2,1)S(1)} %bitcast.5) | data formatting | bytes 245760 | tf_op jit(solution)/shard_map/broadcast_in_dim | solution.py:486

commit v4 on v3

--- a/solution.py
+++ b/solution.py
@@ -142,7 +142,8 @@
         return tiles[b, c]
 
     barrier = pltpu.get_barrier_semaphore()
-    has_before = has_after = True
+    has_before = tm > 0
+    has_after = tm < n_tm - 1
 
     @pl.when(has_before)
     def _():
@@ -164,21 +165,47 @@
     for f in range(2):
         whole = jnp.concatenate([inter[pl.ds(2 + f, CELLS, stride=FR), :], jnp.zeros((ROWS - CELLS, C), F32)], axis=0)
         out_halo[0, f] = whole.astype(BF16)
-    pl.semaphore_wait(barrier, 2 * len(STEPS) + 1)
-
-    sent = {}
-
-    def send(t, k, source, target, device):
-        copy = pltpu.make_async_remote_copy(
+    pl.semaphore_wait(barrier, len(STEPS) + jnp.where(has_after, len(STEPS) + 1, 0))
+
+    def ends(t, k):
+        if k == 8:
+            return out_halo.at[t], halo.at[t]
+        g, k = divmod(k, 9)
+        s = t - 1
+        if t == 0:
+            if k < 2:
+                return vid.at[(TH - 1, 0)[k]], first_row.at[g, k]
+            if k < 4:
+                return vid.at[:, (TW - 1, 0)[k - 2]], first_col.at[g, k - 2]
+            h, c = CORNERS[k - 4]
+            return vid.at[h, pl.ds(c, 1)], first_corner.at[g, 7 - k]
+        if k < 2:
+            return (out_row.at[s, k, 1], next_row.at[s, k]) if g else (out_row.at[s, k], in_row.at[s, k])
+        if k < 4:
+            k = k - 2
+            return (out_col.at[s, k, 1], next_col.at[s, k]) if g else (out_col.at[s, k], in_col.at[s, k])
+        return out_corner.at[s, k - 4], (next_corner if g else in_corner).at[s, 7 - k]
+
+    def message(t, k):
+        source, land = ends(t, k)
+        step = (0, 0) if k == 8 else STEPS[k % 9]
+        return pltpu.make_async_remote_copy(
             src_ref=source,
-            dst_ref=target,
+            dst_ref=land,
             send_sem=send_sem.at[t, k],
             recv_sem=recv_sem.at[t, k],
-            device_id=device,
+            device_id=(tm if k < 8 else after, tile(*step)),
             device_id_type=MESH,
         )
-        copy.start()
-        sent[t, k] = copy
+
+    def send_all(t):
+        for k in range(7, -1, -1):
+            message(t, k).start()
+
+        @pl.when(has_after)
+        def _():
+            for k in (8, 16, 15, 14, 13, 12, 11, 10, 9):
+                message(t, k).start()
 
     def fill(slot, own, top, bottom, left_side, right_side):
         for c in range(3):
@@ -246,22 +273,7 @@
     for t in range(LAYERS):
         s = t - 1
         if t == 0:
-            rims = [vid.at[TH - 1], vid.at[0], vid.at[:, TW - 1], vid.at[:, 0]] + [vid.at[h, pl.ds(c, 1)] for h, c in CORNERS]
-
-            def give(g, where_to, rims=rims):
-                lands = [first_row.at[g, 0], first_row.at[g, 1], first_col.at[g, 0], first_col.at[g, 1]] + [
-                    first_corner.at[g, 3 - k] for k in range(4)
-                ]
-                for k in range(7, -1, -1):
-                    send(0, 9 * g + k, rims[k], lands[k], (where_to, tile(*STEPS[k])))
-
-            give(0, tm)
-
-            @pl.when(has_after)
-            def _(give=give):
-                send(0, 8, out_halo.at[0], halo.at[0], (after, space))
-                give(1, after)
-
+            send_all(0)
         else:
             value = y[s]
             sums = [jnp.sum(value[f], axis=0, keepdims=True) for f in range(FR)]
@@ -307,29 +319,10 @@
             out_row[s] = stage_row[...].astype(BF16)
             out_col[s] = stage_col[...].astype(BF16)
             out_corner[s] = stage_corner[...].astype(BF16)
-            for k in range(7, -1, -1):
-                if k < 2:
-                    source, land = out_row.at[s, k], in_row.at[s, k]
-                elif k < 4:
-                    source, land = out_col.at[s, k - 2], in_col.at[s, k - 2]
-                else:
-                    source, land = out_corner.at[s, k - 4], in_corner.at[s, 7 - k]
-                send(t, k, source, land, (tm, tile(*STEPS[k])))
-
-            @pl.when(has_after)
-            def _(s=s, t=t):
-                send(t, 8, out_halo.at[t], halo.at[t], (after, space))
-                for k in range(7, -1, -1):
-                    if k < 2:
-                        source, land = out_row.at[s, k, 1], next_row.at[s, k]
-                    elif k < 4:
-                        source, land = out_col.at[s, k - 2, 1], next_col.at[s, k - 2]
-                    else:
-                        source, land = out_corner.at[s, k - 4], next_corner.at[s, 7 - k]
-                    send(t, 9 + k, source, land, (after, tile(*STEPS[k])))
+            send_all(t)
 
         for k in range(8):
-            sent[t, k].wait_recv()
+            message(t, k).wait_recv()
         loads[1 + t].wait()
 
         if t == 0:
@@ -377,7 +370,7 @@
         @pl.when(has_before)
         def _(s=s, t=t):
             for k in range(8, 17):
-                sent[t, k].wait_recv()
+                message(t, k).wait_recv()
             if t == 0:
                 pl.semaphore_signal(ready_sem, inc=1, device_id=(before, space), device_id_type=MESH)
             else:
@@ -409,7 +402,7 @@
 
     for t in range(LAYERS):
         for k in range(8):
-            sent[t, k].wait_send()
+            message(t, k).wait_send()
     for s in range(LAYERS - 1):
         pltpu.make_async_copy(slots.at[s], slots.at[s], stat_send.at[s, 0]).wait()
 
@@ -417,7 +410,7 @@
     def _():
         for t in range(LAYERS):
             for k in range(8, 17):
-                sent[t, k].wait_send()
+                message(t, k).wait_send()
         for s in range(LAYERS - 1):
             pltpu.make_async_copy(prev_slots.at[s], prev_slots.at[s], stat_send.at[s, 1]).wait()
 

time: 35.9 us -> 35.1 us (0.978); the launches traced: 35.7 us -> 34.5 us
  Pallas kernels: 35 us -> 33.8 us
    pallas_call x1, Pallas kernels: 35 us -> 33.8 us  [on_device(): pl.pallas_call(kernel, out_shape=jax.ShapeDtypeStruct((FR, TH, TW, C), BF...]
where the time goes in v4:
time: 35.1 us; the launch traced here: 34.5 us
  Pallas kernels  33.8 us (96%)
  local copies, waits for them, and re-layouts  0.7 us (2%)
    pallas_call x1, Pallas kernels, on_device(): pl.pallas_call(kernel, out_shape=jax.ShapeDtypeStruct((FR, TH, TW, C), BF...  33.8 us

profile of v4, /device:TPU:1, one launch (start us, length us, event | category | flops | bytes accessed | tf_op | source)
XLA Modules:
  0.0 34.5 jit_solution(2827618370468207321)
XLA Ops:
  0.0 33.8 %conv_stack.1 = bf16[4,6,20,128]{3,2,1,0:T(8,128)(2,1)S(1)} custom-call(bf16[6,20,4,128]{3,2,1,0:T(4,128)(2,1)} %bitcast.7, bf16[3,3,1152,128]{3,2,1,0:T(8,128)(2,1)} %bitcast.6, f32[2,128]{1,0:T(2,128)} %gain_in.1, f32[2,128]{1,0:T(2,128)} %bias_in.1), custom_call_target="tpu_custom_call" | custom-call | flops 1274019840 | bytes 2900000 | tf_op jit(solution)/shard_map/conv_stack/pallas_call | solution.py:427
  33.8 0.7 %copy.5 = bf16[4,1,6,20,128]{4,0,3,2,1:T(4,128)(2,1)} copy(bf16[4,1,6,20,128]{4,3,2,0,1:T(8,128)(2,1)S(1)} %bitcast.5) | data formatting | bytes 245760 | tf_op jit(solution)/shard_map/broadcast_in_dim | solution.py:479

commit v5 on v4

--- a/solution.py
+++ b/solution.py
@@ -258,7 +258,7 @@
             row_cells[g, i] = first_row[g, i].astype(F32).reshape(FR * TW, C)
             col_cells[g, i, FR : FR * (TH + 1), :] = first_col[g, i].astype(F32).reshape(FR * TH, C)
             col_cells[g, i, 0:FR, :] = first_corner[g, i].astype(F32).reshape(FR, C)
-            col_cells[g, i, FR * (TH + 1) :, :] = first_corner[g, 2 + i].astype(F32).reshape(FR, C)
+            col_cells[g, i, FR * (TH + 1) : FR * (TH + 2), :] = first_corner[g, 2 + i].astype(F32).reshape(FR, C)
 
     def rims_of(p, f):
         lo = f * TW
@@ -275,7 +275,7 @@
         if t == 0:
             send_all(0)
         else:
-            value = y[s]
+            value = y[s, 0:FR]
             sums = [jnp.sum(value[f], axis=0, keepdims=True) for f in range(FR)]
             squares = [jnp.sum(value[f] * value[f], axis=0, keepdims=True) for f in range(FR)]
             packed[s] = pack_sums(jnp.concatenate(sums + squares, axis=0))
@@ -316,9 +316,9 @@
                 if p == 1:
                     whole = jnp.concatenate([y[s, f, 0:CELLS, :] - off, jnp.broadcast_to(off, (ROWS - CELLS, C))], axis=0)
                     out_halo[t, lo] = whole.astype(BF16)
-            out_row[s] = stage_row[...].astype(BF16)
-            out_col[s] = stage_col[...].astype(BF16)
-            out_corner[s] = stage_corner[...].astype(BF16)
+            out_row[s] = stage_row[:, :, 0:48, :].astype(BF16)
+            out_col[s] = stage_col[:, :, 0:16, :].astype(BF16)
+            out_corner[s] = stage_corner[:, :, 0:FR, :].astype(BF16)
             send_all(t)
 
         for k in range(8):
@@ -347,9 +347,9 @@
 
                 return act
 
-            rim_row[...] = in_row[s].astype(F32)
-            rim_col[...] = in_col[s].astype(F32)
-            rim_corner[...] = in_corner[s].astype(F32)
+            rim_row[:, :, 0:48, :] = in_row[s].astype(F32)
+            rim_col[:, :, 0:16, :] = in_col[s].astype(F32)
+            rim_corner[:, :, 0:FR, :] = in_corner[s].astype(F32)
             pltpu.make_async_copy(slots.at[s], slots.at[s], stat_recv.at[s, 0]).wait()
             stats = moments(packed[s] + jnp.sum(slots[s], axis=0), gain)
             for f in range(FR):
@@ -382,9 +382,9 @@
                 frame(f, [(halo[0, f].astype(F32)[0:CELLS],), *split(1, 2 + f)], same, later)
         else:
             for i in range(2):
-                rim_row[i, 1] = next_row[s, i].astype(F32)
-                rim_col[i, 1] = next_col[s, i].astype(F32)
-            rim_corner[...] = next_corner[s].astype(F32)
+                rim_row[i, 1, 0:48, :] = next_row[s, i].astype(F32)
+                rim_col[i, 1, 0:16, :] = next_col[s, i].astype(F32)
+            rim_corner[:, :, 0:FR, :] = next_corner[s].astype(F32)
             stats = moments(jnp.sum(prev_slots[s], axis=0), gain)
             for f in range(2):
                 whole = halo[t, f].astype(F32)
@@ -437,16 +437,16 @@
             pltpu.VMEM((2, 2, TH, FR, C), BF16),
             pltpu.VMEM((2, 4, 1, FR, C), BF16),
             pltpu.VMEM((2, 2, FR * TW, C), F32),
-            pltpu.VMEM((2, 2, FR * (TH + 2), C), F32),
+            pltpu.VMEM((2, 2, FR * (TH + 2) + 8, C), F32),
             pltpu.VMEM((inner, C), F32),
             pltpu.VMEM((inner, C), F32),
-            pltpu.VMEM((inner, FR, ROWS, C), F32),
+            pltpu.VMEM((inner, FR + 1, ROWS, C), F32),
             pltpu.VMEM((FR, ROWS, C), F32),
             pltpu.VMEM((FR + 2, 3, XROWS, C), F32),
             pltpu.VMEM((FR + 2, ROWS, K), BF16),
-            pltpu.VMEM((2, 2, 48, C), F32),
-            pltpu.VMEM((2, 2, 16, C), F32),
-            pltpu.VMEM((4, 2, FR, C), F32),
+            pltpu.VMEM((2, 2, 56, C), F32),
+            pltpu.VMEM((2, 2, 24, C), F32),
+            pltpu.VMEM((4, 2, 16, C), F32),
             pltpu.VMEM((inner, 2, 2, 48, C), BF16),
             pltpu.VMEM((inner, 2, 2, 16, C), BF16),
             pltpu.VMEM((inner, 4, 2, FR, C), BF16),
@@ -458,9 +458,9 @@
             pltpu.VMEM((inner, 2, 16, C), BF16),
             pltpu.VMEM((inner, 4, 2, FR, C), BF16),
             pltpu.VMEM((LAYERS, 2, ROWS, C), BF16),
-            pltpu.VMEM((2, 2, 48, C), F32),
-            pltpu.VMEM((2, 2, 16, C), F32),
-            pltpu.VMEM((4, 2, FR, C), F32),
+            pltpu.VMEM((2, 2, 56, C), F32),
+            pltpu.VMEM((2, 2, 24, C), F32),
+            pltpu.VMEM((4, 2, 16, C), F32),
             pltpu.VMEM((inner, 2, C), F32),
             pltpu.VMEM((inner, n_space - 1, 2, C), F32),
             pltpu.VMEM((inner, n_space, 2, C), F32),

time: 35.1 us -> 35.1 us (level)
  no operation moved by 1% of the time
where the time goes in v5:
time: 35.1 us; the launch traced here: 34.5 us
  Pallas kernels  33.8 us (96%)
  local copies, waits for them, and re-layouts  0.7 us (2%)
    pallas_call x1, Pallas kernels, on_device(): pl.pallas_call(kernel, out_shape=jax.ShapeDtypeStruct((FR, TH, TW, C), BF...  33.8 us

profile of v5, /device:TPU:1, one launch (start us, length us, event | category | flops | bytes accessed | tf_op | source)
XLA Modules:
  0.0 34.5 jit_solution(17718250336496409126)
XLA Ops:
  0.0 33.8 %conv_stack.1 = bf16[4,6,20,128]{3,2,1,0:T(8,128)(2,1)S(1)} custom-call(bf16[6,20,4,128]{3,2,1,0:T(4,128)(2,1)} %bitcast.7, bf16[3,3,1152,128]{3,2,1,0:T(8,128)(2,1)} %bitcast.6, f32[2,128]{1,0:T(2,128)} %gain_in.1, f32[2,128]{1,0:T(2,128)} %bias_in.1), custom_call_target="tpu_custom_call" | custom-call | flops 1274019840 | bytes 2900000 | tf_op jit(solution)/shard_map/conv_stack/pallas_call | solution.py:427
  33.8 0.7 %copy.5 = bf16[4,1,6,20,128]{4,0,3,2,1:T(4,128)(2,1)} copy(bf16[4,1,6,20,128]{4,3,2,0,1:T(8,128)(2,1)S(1)} %bitcast.5) | data formatting | bytes 245760 | tf_op jit(solution)/shard_map/broadcast_in_dim | solution.py:479

commit v6 on v5

--- a/solution.py
+++ b/solution.py
@@ -204,7 +204,7 @@
 
         @pl.when(has_after)
         def _():
-            for k in (8, 16, 15, 14, 13, 12, 11, 10, 9):
+            for k in (16, 15, 14, 13, 12, 11, 10, 9, 8):
                 message(t, k).start()
 
     def fill(slot, own, top, bottom, left_side, right_side):

time: 35.1 us -> 35.2 us (level)
  no operation moved by 1% of the time
where the time goes in v6:
time: 35.2 us; the launch traced here: 34.5 us
  Pallas kernels  33.8 us (96%)
  local copies, waits for them, and re-layouts  0.7 us (2%)
    pallas_call x1, Pallas kernels, on_device(): pl.pallas_call(kernel, out_shape=jax.ShapeDtypeStruct((FR, TH, TW, C), BF...  33.8 us

profile of v6, /device:TPU:1, one launch (start us, length us, event | category | flops | bytes accessed | tf_op | source)
XLA Modules:
  0.0 34.5 jit_solution(11112478876667532491)
XLA Ops:
  0.0 33.8 %conv_stack.1 = bf16[4,6,20,128]{3,2,1,0:T(8,128)(2,1)S(1)} custom-call(bf16[6,20,4,128]{3,2,1,0:T(4,128)(2,1)} %bitcast.7, bf16[3,3,1152,128]{3,2,1,0:T(8,128)(2,1)} %bitcast.6, f32[2,128]{1,0:T(2,128)} %gain_in.1, f32[2,128]{1,0:T(2,128)} %bias_in.1), custom_call_target="tpu_custom_call" | custom-call | flops 1274019840 | bytes 2900000 | tf_op jit(solution)/shard_map/conv_stack/pallas_call | solution.py:427
  33.8 0.7 %copy.5 = bf16[4,1,6,20,128]{4,0,3,2,1:T(4,128)(2,1)} copy(bf16[4,1,6,20,128]{4,3,2,0,1:T(8,128)(2,1)S(1)} %bitcast.5) | data formatting | bytes 245760 | tf_op jit(solution)/shard_map/broadcast_in_dim | solution.py:479
